TPU v7x, 256 devices: a whole 4x4x8 slice. The times are simulated.
256 devices in a mesh: plane: 8 (over z), mode: 32 (over y, x, core).
Axes of the slice: x: 4, y: 4, z: 8, core: 2. Of those that a mesh axis runs over, the one named last changes fastest.
Arguments:
- velocity: float32 [3, 512, 49, 1024], P(None, 'mode', None, 'plane'), may hold values from -8 to 8
- metric_terms: float32 [4, 49, 1024], P(None, None, 'plane'), may hold values from -1.75 to 1.75
- lift_scale: float32 [2, 4, 7, 1024], P(None, None, None, 'plane'), may hold values from -6 to 6
- neighbour: int32 [4, 1024], P(None, 'plane'), may hold values from -1 to 1023, as said below
- neighbour_side: int32 [4, 1024], P(None, 'plane'), may hold values from 0 to 3, as said below
- orientation: int32 [4, 1024], P(None, 'plane'), may hold values from 0 to 1, as said below
Outputs:
- advection: float32 [3, 512, 49, 1024], P(None, 'mode', None, 'plane')
Inputs may be any that keep to these rules, and one draw needn't show every extreme that they name: neighbour[s, e] is the element across side s of element e, or -1 on the domain's boundary; it lies in the same partition of 128 elements as e or in an adjacent one, and the relation is symmetric: neighbour[neighbour_side[s, e], neighbour[s, e]] = e. Partitions p and p + 1 share 20 or 21 sides, partitions 0 and 1 exactly 21. 0 where neighbour is -1; otherwise neighbour_side[neighbour_side[s, e], neighbour[s, e]] = s. `orientation`: 0 where neighbour is -1; the same value seen from both elements of a shared side.
All inputs are finite; a program needn't handle non-finite values.
Results may differ from a plain program's by a relative error of at most 0.000096.
Values sent between devices are 32-bit elements; how exact they have to be, the bound alone decides.
A program may use at most 128 MiB of HBM per device.

v0:
```python
import jax
import jax.numpy as jnp
import ml_dtypes
import numpy as np
from jax import lax
from jax.experimental import pallas as pl
from jax.experimental.pallas import tpu as pltpu
from jax.sharding import PartitionSpec as P

MESH = pl.DeviceIdType.MESH
F32 = jnp.float32
BF16 = jnp.bfloat16

NP = 7
NN = 49
NZ = 512
MODES = 32
PLANES = 8
LOCAL = 16
ELEMS = 128
SPAN_WAVENUMBER = 0.25
VEL_GROUPS = 5
GROUPS = 8

GLL_POINTS = (
    -1.0,
    -0.830223896278567,
    -0.468848793470714,
    0.0,
    0.468848793470714,
    0.830223896278567,
    1.0,
)

PIECES = (
    (0, 0, 0, 32),
    (1, 0, 32, 17),
    (1, 17, 130, 15),
    (2, 0, 49, 32),
    (3, 0, 81, 17),
    (3, 17, 145, 2),
    (4, 0, 98, 32),
)


def derivative_matrix():
    points = np.array(GLL_POINTS)
    identity = np.eye(NP)
    offdiag = points[:, None] - points[None, :] + identity
    weights = 1.0 / np.prod(offdiag, axis=1)
    matrix = weights[None, :] / weights[:, None] / offdiag
    matrix = matrix * (1.0 - identity)
    return matrix - identity * matrix.sum(axis=1)[:, None]


def split_np(table):
    table = table.astype(np.float32)
    high = table.astype(ml_dtypes.bfloat16)
    low = (table - high.astype(np.float32)).astype(ml_dtypes.bfloat16)
    return high, low


def side_node(side, position):
    return (position, position * NP + NP - 1, (NP - 1) * NP + position, position * NP)[side]


def tables():
    index = np.arange(NZ)
    wave = np.where(index == 1, NZ // 2, index // 2)
    phase = (wave[:, None] * index[None, :] % NZ) * (2.0 * np.pi / NZ)
    sine_row = ((index % 2 == 1) & (index > 1))[:, None]
    inverse = np.where(sine_row, np.sin(phase), np.cos(phase))
    slope = np.where(index < 2, 0.0, wave)[:, None] * SPAN_WAVENUMBER
    slope = slope * np.where(sine_row, np.cos(phase), -np.sin(phase))
    weighting = np.where(index < 2, 1.0, 2.0) / NZ
    high, low = split_np(np.concatenate([inverse.T, slope.T], axis=0))
    backward = np.concatenate([high, low, high], axis=1)
    high, low = split_np(inverse * weighting[:, None])
    forward = np.concatenate([high, low, high], axis=1)
    matrix = derivative_matrix()
    derive = np.zeros((256, 512))
    for j in range(NP):
        for i in range(NP):
            for b in range(NP):
                for e in range(4):
                    derive[4 * (j * NP + b) + e, 4 * (j * NP + i) + e] = matrix[i, b]
                    derive[4 * (b * NP + i) + e, 256 + 4 * (j * NP + i) + e] = matrix[j, b]
    high, low = split_np(derive)
    derive = np.concatenate([high, high, low], axis=0)
    place = np.zeros((128, 512))
    for side in range(4):
        for position in range(NP):
            for e in range(4):
                column = 4 * side_node(side, position) + e
                place[4 * (side * NP + position) + e, 256 * (side % 2) + column] = 1.0
    place = place.astype(ml_dtypes.bfloat16)
    return backward, forward, derive, np.concatenate([place, place], axis=0)


def halves(value):
    high = value.astype(BF16)
    return high, (value - high.astype(F32)).astype(BF16)


def lane_swap(load, store):
    lane = lax.broadcasted_iota(jnp.int32, (8, 128), 1)
    tiles = [load(p) for p in range(32)]
    for bit in range(5):
        step = 4 << bit
        mask = (lane & step) != 0
        for p in range(32):
            if p >> bit & 1:
                continue
            q = p | 1 << bit
            a, b = tiles[p], tiles[q]
            tiles[p] = jnp.where(mask, pltpu.roll(b, step, 1), a)
            tiles[q] = jnp.where(mask, b, pltpu.roll(a, 128 - step, 1))
    for d in range(32):
        store(d, tiles[d])


def matmul(a, b):
    return jnp.dot(a, b, preferred_element_type=F32)


def matmul_nt(a, b):
    return lax.dot_general(a, b, (((1,), (1,)), ((), ())), preferred_element_type=F32)


def exact(a, b):
    return jnp.dot(a, b, precision=lax.Precision.HIGHEST, preferred_element_type=F32)


def main_kernel(
    v_hbm,
    metric_hbm,
    lift_hbm,
    nb_hbm,
    ns_hbm,
    or_hbm,
    inv_hbm,
    fwd_hbm,
    der_hbm,
    place_hbm,
    back,
    vn,
    vs,
    sb,
    rx,
    sb2,
    inv,
    fwd,
    der,
    place,
    met,
    lif,
    nbv,
    nsv,
    orv,
    lmat,
    kmat,
    oh,
    sel,
    oht,
    up_out,
    dn_out,
    up_in,
    dn_in,
    rows,
    xr,
    pv,
    dlhs,
    dxe,
    base,
    uu,
    xa,
    la,
    xp,
    tail,
    load_sem,
    in_sem,
    send_sem,
    recv_sem,
    send2_sem,
    recv2_sem,
    halo_send,
    halo_recv,
):
    me = lax.axis_index("mode")
    part = lax.axis_index("plane")
    above = lax.rem(part + 1, PLANES)
    below = lax.rem(part + PLANES - 1, PLANES)

    nbv[...] = jnp.full((8, 128), -1, jnp.int32)
    nsv[...] = jnp.zeros((8, 128), jnp.int32)
    orv[...] = jnp.zeros((8, 128), jnp.int32)
    met[...] = jnp.zeros_like(met)
    lif[...] = jnp.zeros_like(lif)
    loads = []
    for k, (group, slot, row, count) in enumerate(PIECES):
        copy = pltpu.make_async_copy(
            v_hbm.at[pl.ds(row, count)], vs.at[group, pl.ds(slot, count)], load_sem.at[k]
        )
        copy.start()
        loads.append((group, copy))
    others = []
    for k, (src, dst) in enumerate(
        (
            (v_hbm, vn),
            (nb_hbm, nbv.at[pl.ds(0, 4)]),
            (ns_hbm, nsv.at[pl.ds(0, 4)]),
            (or_hbm, orv.at[pl.ds(0, 4)]),
            (metric_hbm, met.at[:, pl.ds(0, 4)]),
            (lift_hbm, lif.at[:, pl.ds(0, 4)]),
            (inv_hbm, inv),
            (der_hbm, der),
            (place_hbm, place),
            (fwd_hbm, fwd),
        )
    ):
        copy = pltpu.make_async_copy(src, dst, in_sem.at[k])
        copy.start()
        others.append(copy)

    barrier = pltpu.get_barrier_semaphore()

    @pl.loop(1, MODES)
    def _(k):
        pl.semaphore_signal(
            barrier, inc=1, device_id={"mode": lax.rem(me + k, MODES)}, device_id_type=MESH
        )

    for other in (above, below):
        pl.semaphore_signal(barrier, inc=1, device_id={"plane": other}, device_id_type=MESH)

    vs[3, pl.ds(19, 13)] = jnp.zeros((13, LOCAL, 128), F32)
    for comp in range(3):
        vs[VEL_GROUPS + comp, pl.ds(28, 4)] = jnp.zeros((4, LOCAL, 128), F32)

    def scatter(group):
        @pl.loop(0, 2)
        def _(half):
            rows8 = pl.ds(pl.multiple_of(half * 8, 8), 8)

            def store(d, tile):
                sb[group, d, rows8] = tile

            lane_swap(lambda p: vs[group, p, rows8], store)

    def send(group):
        mine = rx.at[group, pl.ds(pl.multiple_of(me * LOCAL, LOCAL), LOCAL)]
        pltpu.make_async_copy(sb.at[group, me], mine, recv_sem.at[group]).start()

        @pl.loop(1, MODES)
        def _(k):
            to = lax.rem(me + k, MODES)
            pltpu.make_async_remote_copy(
                src_ref=sb.at[group, to],
                dst_ref=mine,
                send_sem=send_sem.at[group],
                recv_sem=recv_sem.at[group],
                device_id={"mode": to},
                device_id_type=MESH,
            ).start()

    for group in range(VEL_GROUPS):
        for owner, copy in loads:
            if owner == group:
                copy.wait()
        scatter(group)
        if group == 0:
            pl.semaphore_wait(barrier, MODES + 1)
        send(group)

    for copy in others[:4]:
        copy.wait()
    nb = nbv[...]
    exists = nb >= 0
    owner = lax.shift_right_arithmetic(nb, 7)
    target = nsv[...] * ELEMS + (nb & (ELEMS - 1))
    own_key = jnp.where(exists & (owner == part), target, -1)
    is_up = exists & (owner == part + 1)
    is_dn = exists & (owner == part - 1)
    strict = (
        lax.broadcasted_iota(jnp.int32, (128, 128), 0)
        < lax.broadcasted_iota(jnp.int32, (128, 128), 1)
    ).astype(F32)
    ranks = []
    for border in (is_up, is_dn):
        flag = jnp.where(border, 1.0, 0.0)
        before = exact(flag, strict)
        totals = jnp.sum(flag, axis=1, keepdims=True)
        offset = jnp.zeros((1, 1), F32)
        out = []
        for side in range(4):
            out.append(before[side : side + 1] + offset)
            offset = offset + totals[side : side + 1]
        ranks.append(out)
    row128 = lax.broadcasted_iota(jnp.int32, (128, 128), 0).astype(F32)
    row512 = lax.broadcasted_iota(jnp.int32, (512, 128), 0)
    for side in range(4):
        lanes = pl.ds(side * 128, 128)
        one = slice(side, side + 1)
        slot = jnp.where(
            is_up[one], ranks[0][side], jnp.where(is_dn[one], 32.0 + ranks[1][side], -1.0)
        )
        sel[:, lanes] = jnp.where(row128 == slot, 1.0, 0.0).astype(BF16)
        oh[:, lanes] = jnp.where(row512 == own_key[one], 1.0, 0.0).astype(BF16)
        high, low = halves(jnp.broadcast_to((target[one] + 1).astype(F32), (16, 128)))
        kmat[pl.ds(0, 16), lanes] = high
        kmat[pl.ds(16, 16), lanes] = low
    turned = orv[...] == 1

    @pl.loop(0, 3)
    def _(comp):
        for position in range(NP):
            for side in range(4):
                straight = vn[comp * NN + side_node(side, position)]
                reverse = vn[comp * NN + side_node(side, NP - 1 - position)]
                value = jnp.where(turned[side : side + 1], reverse, straight)
                high, low = halves(value)
                lanes = pl.ds(side * 128, 128)
                lmat[comp, pl.ds(position * 16, 16), lanes] = high
                lmat[comp, pl.ds(112 + position * 16, 16), lanes] = low

    picked = []
    for comp in range(3):
        both = matmul_nt(lmat[comp], sel[...])
        picked.append(both[:112] + both[112:])
    both = matmul_nt(kmat[...], sel[...])
    keys = jnp.concatenate([both[:16] + both[16:], jnp.zeros((96, 128), F32)], axis=0)
    picked.append(keys)
    lane = lax.broadcasted_iota(jnp.int32, (112, 128), 1)
    for ref, shift in ((up_out, 0), (dn_out, 96)):
        packed = None
        for k in (3, 2, 1, 0):
            by = (32 * k + shift) % 128
            moved = pltpu.roll(picked[k], by, 1) if by else picked[k]
            packed = moved if packed is None else jnp.where(lane < 32 * k + 32, moved, packed)
        ref[...] = packed
    halo = []
    for k, (src, dst, to) in enumerate(((up_out, up_in, above), (dn_out, dn_in, below))):
        copy = pltpu.make_async_remote_copy(
            src_ref=src,
            dst_ref=dst,
            send_sem=halo_send.at[k],
            recv_sem=halo_recv.at[k],
            device_id={"plane": to},
            device_id_type=MESH,
        )
        copy.start()
        halo.append(copy)

    for copy in others[4:6]:
        copy.wait()
    fold = (
        lax.broadcasted_iota(jnp.int32, (128, 256), 0)
        == 4 * me + (lax.broadcasted_iota(jnp.int32, (128, 256), 1) & 3)
    ).astype(F32)
    spread = exact(met[...].reshape(NN * 8, 128), fold).reshape(NN, 8, 256)
    node3 = lax.shift_right_arithmetic(lax.broadcasted_iota(jnp.int32, (NN, 8, 256), 2), 2)
    here = node3 == lax.broadcasted_iota(jnp.int32, (NN, 8, 256), 0)
    metric_rows = jnp.sum(jnp.where(here, spread, 0.0), axis=0)
    rows[pl.ds(0, 4)] = metric_rows[:4]
    live = exact(jnp.where(exists, 0.5, 0.0), fold)
    spread = exact(lif[...].reshape(2 * NP * 8, 128), fold).reshape(2 * NP, 8, 256)
    node2 = lax.shift_right_arithmetic(lax.broadcasted_iota(jnp.int32, (8, 256), 1), 2)
    side2 = lax.broadcasted_iota(jnp.int32, (8, 256), 0)
    for axis in range(2):
        total = jnp.zeros((8, 256), F32)
        for position in range(NP):
            wanted = jnp.full((8, 256), -1, jnp.int32)
            for side in range(4):
                wanted = jnp.where(side2 == side, side_node(side, position), wanted)
            total = total + jnp.where(node2 == wanted, spread[axis * NP + position], 0.0)
        total = total * live
        rows[pl.ds(4 + axis, 1)] = total[0:1] + total[2:3]
        rows[pl.ds(6 + axis, 1)] = total[1:2] + total[3:4]

    for copy in halo:
        copy.wait_recv()
    lane1 = lax.broadcasted_iota(jnp.int32, (8, 128), 1)
    key_up = pltpu.roll(up_in[pl.ds(0, 8)], 32, 1)
    key_dn = pltpu.roll(dn_in[pl.ds(0, 8)], 64, 1)
    key = jnp.where(lane1 < 32, key_up, jnp.where(lane1 < 64, key_dn, 0.0))[0:1]
    oht[...] = jnp.where((row512 + 1).astype(F32) == key, 1.0, 0.0).astype(BF16)
    for comp in range(3):
        both = matmul(lmat[comp], oh[...])
        across = both[:112] + both[112:]
        from_up = pltpu.roll(up_in[...], (128 - 32 * comp) % 128, 1) if comp else up_in[...]
        from_dn = pltpu.roll(dn_in[...], (160 - 32 * comp) % 128, 1) if comp != 1 else dn_in[...]
        high, low = halves(jnp.where(lane < 32, from_up, jnp.where(lane < 64, from_dn, 0.0)))
        both = matmul_nt(jnp.concatenate([high, low], axis=0), oht[...])
        across = across + (both[:112] + both[112:])
        for side in range(4):
            for position in range(NP):
                vs[VEL_GROUPS + comp, side * NP + position] = across[
                    position * 16 : position * 16 + 16, side * 128 : side * 128 + 128
                ]
        scatter(VEL_GROUPS + comp)
        send(VEL_GROUPS + comp)

    def received(group):
        pltpu.make_async_copy(rx.at[group], rx.at[group], recv_sem.at[group]).wait()

    for copy in others[6:]:
        copy.wait()
    for group in range(VEL_GROUPS):
        received(group)
    lane64 = lax.broadcasted_iota(jnp.int32, (64, 128), 1)

    @pl.loop(0, 8)
    def _(block):
        at = pl.multiple_of(block * 64, 64)
        rows64 = pl.ds(at, 64)
        g1, g3 = rx[1, rows64], rx[3, rows64]
        last = jnp.where(lane64 < 60, pltpu.roll(g1, 60, 1), pltpu.roll(g3, 120, 1))
        pieces = ((rx[0, rows64], g1), (rx[2, rows64], g3), (rx[4, rows64], last))
        for comp in range(3):
            for k in range(2):
                high, low = halves(pieces[comp][k])
                lanes = pl.ds(k * 128, 128)
                xr[comp, rows64, lanes] = high
                xr[comp, pl.ds(at + 512, 64), lanes] = high
                xr[comp, pl.ds(at + 1024, 64), lanes] = low

    @pl.loop(0, 3)
    def _(comp):
        pv[comp] = matmul(inv[...], xr[comp])

    @pl.loop(0, 8)
    def _(block):
        rows64 = pl.ds(pl.multiple_of(block * 64, 64), 64)
        u, v = pv[0, rows64], pv[1, rows64]
        for k in range(4):
            first, second = ((0, 1), (2, 3), (4, 5), (6, 7))[k]
            uu[k, rows64] = u * rows[pl.ds(first, 1)] + v * rows[pl.ds(second, 1)]

    @pl.loop(0, 3)
    def _(comp):
        @pl.loop(0, 8)
        def _(block):
            rows64 = pl.ds(pl.multiple_of(block * 64, 64), 64)
            high, low = halves(pv[comp, rows64])
            dlhs[rows64, pl.ds(0, 256)] = high
            dlhs[rows64, pl.ds(256, 256)] = low
            dlhs[rows64, pl.ds(512, 256)] = high

        dxe[...] = matmul(dlhs[...], der[...])

        @pl.loop(0, 8)
        def _(block):
            at = pl.multiple_of(block * 64, 64)
            rows64 = pl.ds(at, 64)
            total = uu[0, rows64] * dxe[rows64, pl.ds(0, 256)]
            total = total + uu[1, rows64] * dxe[rows64, pl.ds(256, 256)]
            total = total + pv[2, rows64] * pv[comp, pl.ds(at + 512, 64)]
            base[comp, rows64] = total - (uu[2, rows64] + uu[3, rows64]) * pv[comp, rows64]

    def send_back(group):
        pltpu.make_async_copy(
            sb2.at[group, pl.ds(pl.multiple_of(me * LOCAL, LOCAL), LOCAL)],
            back.at[group, me],
            recv2_sem.at[group],
        ).start()

        @pl.loop(1, MODES)
        def _(k):
            to = lax.rem(me + k, MODES)
            pltpu.make_async_remote_copy(
                src_ref=sb2.at[group, pl.ds(pl.multiple_of(to * LOCAL, LOCAL), LOCAL)],
                dst_ref=back.at[group, me],
                send_sem=send2_sem.at[group],
                recv_sem=recv2_sem.at[group],
                device_id={"mode": to},
                device_id_type=MESH,
            ).start()

    @pl.loop(0, 3)
    def _(comp):
        received(VEL_GROUPS + comp)

        @pl.loop(0, 8)
        def _(block):
            at = pl.multiple_of(block * 64, 64)
            high, low = halves(rx[VEL_GROUPS + comp, pl.ds(at, 64)])
            xa[pl.ds(at, 64)] = high
            xa[pl.ds(at + 512, 64)] = high
            xa[pl.ds(at + 1024, 64)] = low

        high, low = halves(matmul(inv[pl.ds(0, 512)], xa[...]))
        la[:, pl.ds(0, 128)] = high
        la[:, pl.ds(128, 128)] = low
        dxe[...] = matmul(la[...], place[...])

        @pl.loop(0, 8)
        def _(block):
            at = pl.multiple_of(block * 64, 64)
            rows64 = pl.ds(at, 64)
            total = base[comp, rows64] + uu[2, rows64] * dxe[rows64, pl.ds(0, 256)]
            total = total + uu[3, rows64] * dxe[rows64, pl.ds(256, 256)]
            high, low = halves(total)
            xp[rows64] = high
            xp[pl.ds(at + 512, 64)] = high
            xp[pl.ds(at + 1024, 64)] = low

        result = matmul(fwd[...], xp[...])
        sb2[2 * comp] = result[:, :128]
        tail[comp] = result[:, 128:]
        send_back(2 * comp)

    @pl.loop(0, 8)
    def _(block):
        rows64 = pl.ds(pl.multiple_of(block * 64, 64), 64)
        last = tail[2, rows64]
        sb2[1, rows64] = jnp.where(lane64 < 68, tail[0, rows64], pltpu.roll(last, 68, 1))
        sb2[3, rows64] = jnp.where(lane64 < 68, tail[1, rows64], pltpu.roll(last, 8, 1))

    send_back(1)
    send_back(3)

    for copy in halo:
        copy.wait_send()
    for group in range(GROUPS):
        sent = sb.at[group, pl.ds(0, MODES - 1)]
        pltpu.make_async_copy(sent, sent, send_sem.at[group]).wait()
    for group in range(VEL_GROUPS):
        sent = sb2.at[group, pl.ds(0, (MODES - 1) * LOCAL)]
        pltpu.make_async_copy(sent, sent, send2_sem.at[group]).wait()
    for group in range(VEL_GROUPS):
        pltpu.make_async_copy(back.at[group], back.at[group], recv2_sem.at[group]).wait()


def last_kernel(back, out, blocks, done, in_sem, out_sem):
    copies = []
    for group in range(VEL_GROUPS):
        copy = pltpu.make_async_copy(back.at[group], blocks.at[group], in_sem.at[group])
        copy.start()
        copies.append(copy)
    leaving = []
    for group in range(VEL_GROUPS):
        copies[group].wait()

        @pl.loop(0, 2)
        def _(half):
            rows8 = pl.ds(pl.multiple_of(half * 8, 8), 8)

            def store(d, tile):
                done[group, d, rows8] = tile

            lane_swap(lambda p: blocks[group, p, rows8], store)

        for k, (owner, slot, row, count) in enumerate(PIECES):
            if owner == group:
                copy = pltpu.make_async_copy(
                    done.at[group, pl.ds(slot, count)], out.at[pl.ds(row, count)], out_sem.at[k]
                )
                copy.start()
                leaving.append(copy)
    for copy in leaving:
        copy.wait()


def shards(velocity, metric_terms, lift_scale, neighbour, neighbour_side, orientation):
    v = jnp.transpose(velocity, (0, 2, 1, 3)).reshape(3 * NN, LOCAL, ELEMS)
    metric = jnp.transpose(metric_terms, (1, 0, 2))
    lift = jnp.transpose(lift_scale, (0, 2, 1, 3)).reshape(2 * NP, 4, ELEMS)
    consts = [jnp.asarray(t) for t in tables()]
    anywhere = pl.BlockSpec(memory_space=pl.ANY)
    vmem = pltpu.VMEM
    dma = pltpu.SemaphoreType.DMA
    back = pl.pallas_call(
        main_kernel,
        out_shape=jax.ShapeDtypeStruct((VEL_GROUPS, MODES, LOCAL, 128), F32),
        in_specs=[anywhere] * 10,
        out_specs=anywhere,
        scratch_shapes=[
            vmem((3 * NN, LOCAL, 128), F32),
            vmem((GROUPS, 32, LOCAL, 128), F32),
            vmem((GROUPS, MODES, LOCAL, 128), F32),
            vmem((GROUPS, NZ, 128), F32),
            vmem((VEL_GROUPS, NZ, 128), F32),
            vmem((2 * NZ, 3 * NZ), BF16),
            vmem((NZ, 3 * NZ), BF16),
            vmem((768, 512), BF16),
            vmem((256, 512), BF16),
            vmem((NN, 8, 128), F32),
            vmem((2 * NP, 8, 128), F32),
            vmem((8, 128), jnp.int32),
            vmem((8, 128), jnp.int32),
            vmem((8, 128), jnp.int32),
            vmem((3, 224, 512), BF16),
            vmem((32, 512), BF16),
            vmem((512, 512), BF16),
            vmem((128, 512), BF16),
            vmem((512, 128), BF16),
            vmem((112, 128), F32),
            vmem((112, 128), F32),
            vmem((112, 128), F32),
            vmem((112, 128), F32),
            vmem((8, 256), F32),
            vmem((3, 3 * NZ, 256), BF16),
            vmem((3, 2 * NZ, 256), F32),
            vmem((NZ, 768), BF16),
            vmem((NZ, 512), F32),
            vmem((3, NZ, 256), F32),
            vmem((4, NZ, 256), F32),
            vmem((3 * NZ, 128), BF16),
            vmem((NZ, 256), BF16),
            vmem((3 * NZ, 256), BF16),
            vmem((3, NZ, 128), F32),
            dma((len(PIECES),)),
            dma((10,)),
            dma((GROUPS,)),
            dma((GROUPS,)),
            dma((VEL_GROUPS,)),
            dma((VEL_GROUPS,)),
            dma((2,)),
            dma((2,)),
        ],
        compiler_params=pltpu.CompilerParams(
            collective_id=0, has_side_effects=True, vmem_limit_bytes=62 << 20
        ),
        name="advect",
    )(v, metric, lift, neighbour, neighbour_side, orientation, *consts)
    out = pl.pallas_call(
        last_kernel,
        out_shape=jax.ShapeDtypeStruct((3 * NN, LOCAL, ELEMS), F32),
        in_specs=[anywhere],
        out_specs=anywhere,
        scratch_shapes=[
            vmem((VEL_GROUPS, MODES, LOCAL, 128), F32),
            vmem((VEL_GROUPS, 32, LOCAL, 128), F32),
            dma((VEL_GROUPS,)),
            dma((len(PIECES),)),
        ],
        compiler_params=pltpu.CompilerParams(vmem_limit_bytes=62 << 20),
        name="restore",
    )(back)
    return jnp.transpose(out.reshape(3, NN, LOCAL, ELEMS), (0, 2, 1, 3))


def solution(mesh):
    return jax.shard_map(
        shards,
        mesh=mesh,
        in_specs=(
            P(None, "mode", None, "plane"),
            P(None, None, "plane"),
            P(None, None, None, "plane"),
            P(None, "plane"),
            P(None, "plane"),
            P(None, "plane"),
        ),
        out_specs=P(None, "mode", None, "plane"),
        check_vma=False,
    )
```

profile of v0, /device:TPU:1, one launch (start us, length us, event | category | flops | bytes accessed | tf_op | source)
XLA Modules:
  0.0 59.7 jit_solution(13770645948243902249)
XLA Ops:
  0.0 53.9 %advect.1.back = f32[5,32,16,128]{3,2,1,0:T(8,128)} custom-call(f32[147,16,128]{2,1,0:T(8,128)} %bitcast.10, f32[49,4,128]{2,1,0:T(4,128)} %bitcast.11, f32[14,4,128]{2,1,0:T(4,128)} %bitcast.12, s32[4,128]{1,0:T(4,128)} %nb_hbm.1, s32[4,128]{1,0:T(4,128)} %ns_hbm.1, s32[4,128]{1,0:T(4,128)} %or_hbm.1, bf16[1024,1536]{1,0:T(8,128)(2,1)} %constant.8.clone.inv_hbm, ...), custom_call_target="tpu_custom_call" | custom-call | tf_op jit(solution)/shard_map/advect/pallas_call | solution.py:572
  53.9 5.8 %restore.1 = f32[147,16,128]{2,1,0:T(8,128)} custom-call(f32[5,32,16,128]{3,2,1,0:T(8,128)} %advect.1.back), custom_call_target="tpu_custom_call" | custom-call | tf_op jit(solution)/shard_map/restore/pallas_call | solution.py:626
where the time goes:
time: 59.8 us; the launch traced here: 59.7 us
  Pallas kernels  59.7 us (100%)
    pallas_call x1, Pallas kernels, shards(): pl.pallas_call(main_kernel, out_shape=jax.ShapeDtypeStruct((VEL_GROUPS, M...  53.9 us
    pallas_call x1, Pallas kernels, shards(): pl.pallas_call(last_kernel, out_shape=jax.ShapeDtypeStruct((3 * NN, LOCAL...  5.81 us

commit v1 on v0

--- a/solution.py
+++ b/solution.py
@@ -72,10 +72,9 @@
     inverse = np.where(sine_row, np.sin(phase), np.cos(phase))
     slope = np.where(index < 2, 0.0, wave)[:, None] * SPAN_WAVENUMBER
     slope = slope * np.where(sine_row, np.cos(phase), -np.sin(phase))
-    weighting = np.where(index < 2, 1.0, 2.0) / NZ
     high, low = split_np(np.concatenate([inverse.T, slope.T], axis=0))
     backward = np.concatenate([high, low, high], axis=1)
-    high, low = split_np(inverse * weighting[:, None])
+    high, low = split_np(inverse)
     forward = np.concatenate([high, low, high], axis=1)
     matrix = derivative_matrix()
     derive = np.zeros((256, 512))
@@ -104,19 +103,14 @@
 
 def lane_swap(load, store):
     lane = lax.broadcasted_iota(jnp.int32, (8, 128), 1)
-    tiles = [load(p) for p in range(32)]
+    tiles = [None] * 32
+    for p in range(32):
+        tiles[-p % 32] = pltpu.roll(load(p), 4 * p, 1) if p else load(p)
     for bit in range(5):
-        step = 4 << bit
-        mask = (lane & step) != 0
-        for p in range(32):
-            if p >> bit & 1:
-                continue
-            q = p | 1 << bit
-            a, b = tiles[p], tiles[q]
-            tiles[p] = jnp.where(mask, pltpu.roll(b, step, 1), a)
-            tiles[q] = jnp.where(mask, b, pltpu.roll(a, 128 - step, 1))
+        mask = (lane & (4 << bit)) != 0
+        tiles = [jnp.where(mask, tiles[(j - (1 << bit)) % 32], tiles[j]) for j in range(32)]
     for d in range(32):
-        store(d, tiles[d])
+        store(d, pltpu.roll(tiles[d], 128 - 4 * d, 1) if d else tiles[d])
 
 
 def matmul(a, b):
@@ -142,7 +136,9 @@
     fwd_hbm,
     der_hbm,
     place_hbm,
+    out,
     back,
+    done,
     vn,
     vs,
     sb,
@@ -185,6 +181,7 @@
     recv2_sem,
     halo_send,
     halo_recv,
+    out_sem,
 ):
     me = lax.axis_index("mode")
     part = lax.axis_index("plane")
@@ -291,11 +288,11 @@
         before = exact(flag, strict)
         totals = jnp.sum(flag, axis=1, keepdims=True)
         offset = jnp.zeros((1, 1), F32)
-        out = []
+        found = []
         for side in range(4):
-            out.append(before[side : side + 1] + offset)
+            found.append(before[side : side + 1] + offset)
             offset = offset + totals[side : side + 1]
-        ranks.append(out)
+        ranks.append(found)
     row128 = lax.broadcasted_iota(jnp.int32, (128, 128), 0).astype(F32)
     row512 = lax.broadcasted_iota(jnp.int32, (512, 128), 0)
     for side in range(4):
@@ -405,39 +402,21 @@
 
     for copy in others[6:]:
         copy.wait()
-    for group in range(VEL_GROUPS):
-        received(group)
     lane64 = lax.broadcasted_iota(jnp.int32, (64, 128), 1)
 
-    @pl.loop(0, 8)
-    def _(block):
-        at = pl.multiple_of(block * 64, 64)
-        rows64 = pl.ds(at, 64)
-        g1, g3 = rx[1, rows64], rx[3, rows64]
-        last = jnp.where(lane64 < 60, pltpu.roll(g1, 60, 1), pltpu.roll(g3, 120, 1))
-        pieces = ((rx[0, rows64], g1), (rx[2, rows64], g3), (rx[4, rows64], last))
-        for comp in range(3):
+    def on_planes(comp, pieces):
+        @pl.loop(0, 8)
+        def _(block):
+            at = pl.multiple_of(block * 64, 64)
             for k in range(2):
-                high, low = halves(pieces[comp][k])
+                high, low = halves(pieces[k](pl.ds(at, 64)))
                 lanes = pl.ds(k * 128, 128)
-                xr[comp, rows64, lanes] = high
-                xr[comp, pl.ds(at + 512, 64), lanes] = high
-                xr[comp, pl.ds(at + 1024, 64), lanes] = low
-
-    @pl.loop(0, 3)
-    def _(comp):
-        pv[comp] = matmul(inv[...], xr[comp])
-
-    @pl.loop(0, 8)
-    def _(block):
-        rows64 = pl.ds(pl.multiple_of(block * 64, 64), 64)
-        u, v = pv[0, rows64], pv[1, rows64]
-        for k in range(4):
-            first, second = ((0, 1), (2, 3), (4, 5), (6, 7))[k]
-            uu[k, rows64] = u * rows[pl.ds(first, 1)] + v * rows[pl.ds(second, 1)]
-
-    @pl.loop(0, 3)
-    def _(comp):
+                xr[pl.ds(at, 64), lanes] = high
+                xr[pl.ds(at + 512, 64), lanes] = high
+                xr[pl.ds(at + 1024, 64), lanes] = low
+
+        pv[comp] = matmul(inv[...], xr[...])
+
         @pl.loop(0, 8)
         def _(block):
             rows64 = pl.ds(pl.multiple_of(block * 64, 64), 64)
@@ -446,16 +425,39 @@
             dlhs[rows64, pl.ds(256, 256)] = low
             dlhs[rows64, pl.ds(512, 256)] = high
 
-        dxe[...] = matmul(dlhs[...], der[...])
-
-        @pl.loop(0, 8)
-        def _(block):
-            at = pl.multiple_of(block * 64, 64)
-            rows64 = pl.ds(at, 64)
-            total = uu[0, rows64] * dxe[rows64, pl.ds(0, 256)]
-            total = total + uu[1, rows64] * dxe[rows64, pl.ds(256, 256)]
-            total = total + pv[2, rows64] * pv[comp, pl.ds(at + 512, 64)]
-            base[comp, rows64] = total - (uu[2, rows64] + uu[3, rows64]) * pv[comp, rows64]
+        dxe[comp] = matmul(dlhs[...], der[...])
+
+    def joined(rows64):
+        return jnp.where(
+            lane64 < 60, pltpu.roll(rx[1, rows64], 60, 1), pltpu.roll(rx[3, rows64], 120, 1)
+        )
+
+    received(0)
+    received(1)
+    on_planes(0, (lambda r: rx[0, r], lambda r: rx[1, r]))
+    received(2)
+    received(3)
+    on_planes(1, (lambda r: rx[2, r], lambda r: rx[3, r]))
+    received(4)
+    on_planes(2, (lambda r: rx[4, r], joined))
+
+    @pl.loop(0, 16)
+    def _(block):
+        at = pl.multiple_of(block * 32, 32)
+        rows32 = pl.ds(at, 32)
+        u, v, w = pv[0, rows32], pv[1, rows32], pv[2, rows32]
+        first = u * rows[pl.ds(0, 1)] + v * rows[pl.ds(1, 1)]
+        second = u * rows[pl.ds(2, 1)] + v * rows[pl.ds(3, 1)]
+        layer_a = u * rows[pl.ds(4, 1)] + v * rows[pl.ds(5, 1)]
+        layer_b = u * rows[pl.ds(6, 1)] + v * rows[pl.ds(7, 1)]
+        uu[0, rows32] = layer_a
+        uu[1, rows32] = layer_b
+        layer_b = layer_a + layer_b
+        for comp in range(3):
+            total = first * dxe[comp, rows32, pl.ds(0, 256)]
+            total = total + second * dxe[comp, rows32, pl.ds(256, 256)]
+            total = total + w * pv[comp, pl.ds(at + 512, 32)]
+            base[comp, rows32] = total - layer_b * pv[comp, rows32]
 
     def send_back(group):
         pltpu.make_async_copy(
@@ -491,14 +493,14 @@
         high, low = halves(matmul(inv[pl.ds(0, 512)], xa[...]))
         la[:, pl.ds(0, 128)] = high
         la[:, pl.ds(128, 128)] = low
-        dxe[...] = matmul(la[...], place[...])
+        dxe[0] = matmul(la[...], place[...])
 
         @pl.loop(0, 8)
         def _(block):
             at = pl.multiple_of(block * 64, 64)
             rows64 = pl.ds(at, 64)
-            total = base[comp, rows64] + uu[2, rows64] * dxe[rows64, pl.ds(0, 256)]
-            total = total + uu[3, rows64] * dxe[rows64, pl.ds(256, 256)]
+            total = base[comp, rows64] + uu[0, rows64] * dxe[0, rows64, pl.ds(0, 256)]
+            total = total + uu[1, rows64] * dxe[0, rows64, pl.ds(256, 256)]
             high, low = halves(total)
             xp[rows64] = high
             xp[pl.ds(at + 512, 64)] = high
@@ -518,6 +520,27 @@
 
     send_back(1)
     send_back(3)
+
+    leaving = []
+    for group in (0, 2, 4, 1, 3):
+        pltpu.make_async_copy(back.at[group], back.at[group], recv2_sem.at[group]).wait()
+
+        @pl.loop(0, 2)
+        def _(half):
+            rows8 = pl.ds(pl.multiple_of(half * 8, 8), 8)
+
+            def store(d, tile):
+                done[group, d, rows8] = tile
+
+            lane_swap(lambda p: back[group, p, rows8], store)
+
+        for k, (owner, slot, row, count) in enumerate(PIECES):
+            if owner == group:
+                copy = pltpu.make_async_copy(
+                    done.at[group, pl.ds(slot, count)], out.at[pl.ds(row, count)], out_sem.at[k]
+                )
+                copy.start()
+                leaving.append(copy)
 
     for copy in halo:
         copy.wait_send()
@@ -527,36 +550,6 @@
     for group in range(VEL_GROUPS):
         sent = sb2.at[group, pl.ds(0, (MODES - 1) * LOCAL)]
         pltpu.make_async_copy(sent, sent, send2_sem.at[group]).wait()
-    for group in range(VEL_GROUPS):
-        pltpu.make_async_copy(back.at[group], back.at[group], recv2_sem.at[group]).wait()
-
-
-def last_kernel(back, out, blocks, done, in_sem, out_sem):
-    copies = []
-    for group in range(VEL_GROUPS):
-        copy = pltpu.make_async_copy(back.at[group], blocks.at[group], in_sem.at[group])
-        copy.start()
-        copies.append(copy)
-    leaving = []
-    for group in range(VEL_GROUPS):
-        copies[group].wait()
-
-        @pl.loop(0, 2)
-        def _(half):
-            rows8 = pl.ds(pl.multiple_of(half * 8, 8), 8)
-
-            def store(d, tile):
-                done[group, d, rows8] = tile
-
-            lane_swap(lambda p: blocks[group, p, rows8], store)
-
-        for k, (owner, slot, row, count) in enumerate(PIECES):
-            if owner == group:
-                copy = pltpu.make_async_copy(
-                    done.at[group, pl.ds(slot, count)], out.at[pl.ds(row, count)], out_sem.at[k]
-                )
-                copy.start()
-                leaving.append(copy)
     for copy in leaving:
         copy.wait()
 
@@ -565,16 +558,19 @@
     v = jnp.transpose(velocity, (0, 2, 1, 3)).reshape(3 * NN, LOCAL, ELEMS)
     metric = jnp.transpose(metric_terms, (1, 0, 2))
     lift = jnp.transpose(lift_scale, (0, 2, 1, 3)).reshape(2 * NP, 4, ELEMS)
-    consts = [jnp.asarray(t) for t in tables()]
+    operands = [v, metric, lift, neighbour, neighbour_side, orientation]
+    operands += [jnp.asarray(t) for t in tables()]
     anywhere = pl.BlockSpec(memory_space=pl.ANY)
     vmem = pltpu.VMEM
     dma = pltpu.SemaphoreType.DMA
-    back = pl.pallas_call(
+    out = pl.pallas_call(
         main_kernel,
-        out_shape=jax.ShapeDtypeStruct((VEL_GROUPS, MODES, LOCAL, 128), F32),
+        out_shape=pltpu.VMEM((3 * NN, LOCAL, ELEMS), F32),
         in_specs=[anywhere] * 10,
         out_specs=anywhere,
         scratch_shapes=[
+            vmem((VEL_GROUPS, MODES, LOCAL, 128), F32),
+            vmem((VEL_GROUPS, 32, LOCAL, 128), F32),
             vmem((3 * NN, LOCAL, 128), F32),
             vmem((GROUPS, 32, LOCAL, 128), F32),
             vmem((GROUPS, MODES, LOCAL, 128), F32),
@@ -599,12 +595,12 @@
             vmem((112, 128), F32),
             vmem((112, 128), F32),
             vmem((8, 256), F32),
-            vmem((3, 3 * NZ, 256), BF16),
+            vmem((3 * NZ, 256), BF16),
             vmem((3, 2 * NZ, 256), F32),
             vmem((NZ, 768), BF16),
-            vmem((NZ, 512), F32),
+            vmem((3, NZ, 512), F32),
             vmem((3, NZ, 256), F32),
-            vmem((4, NZ, 256), F32),
+            vmem((2, NZ, 256), F32),
             vmem((3 * NZ, 128), BF16),
             vmem((NZ, 256), BF16),
             vmem((3 * NZ, 256), BF16),
@@ -617,27 +613,17 @@
             dma((VEL_GROUPS,)),
             dma((2,)),
             dma((2,)),
+            dma((len(PIECES),)),
         ],
         compiler_params=pltpu.CompilerParams(
-            collective_id=0, has_side_effects=True, vmem_limit_bytes=62 << 20
+            collective_id=0, has_side_effects=True, vmem_limit_bytes=48 << 20
         ),
         name="advect",
-    )(v, metric, lift, neighbour, neighbour_side, orientation, *consts)
-    out = pl.pallas_call(
-        last_kernel,
-        out_shape=jax.ShapeDtypeStruct((3 * NN, LOCAL, ELEMS), F32),
-        in_specs=[anywhere],
-        out_specs=anywhere,
-        scratch_shapes=[
-            vmem((VEL_GROUPS, MODES, LOCAL, 128), F32),
-            vmem((VEL_GROUPS, 32, LOCAL, 128), F32),
-            dma((VEL_GROUPS,)),
-            dma((len(PIECES),)),
-        ],
-        compiler_params=pltpu.CompilerParams(vmem_limit_bytes=62 << 20),
-        name="restore",
-    )(back)
-    return jnp.transpose(out.reshape(3, NN, LOCAL, ELEMS), (0, 2, 1, 3))
+    )(*[pltpu.with_memory_space_constraint(x, pltpu.HBM) for x in operands])
+    index = lax.axis_index("mode") * LOCAL + jnp.arange(LOCAL, dtype=jnp.int32)
+    weighting = jnp.where(index < 2, 1.0 / NZ, 2.0 / NZ).astype(F32)
+    out = out.reshape(3, NN, LOCAL, ELEMS) * weighting[:, None]
+    return jnp.transpose(out, (0, 2, 1, 3))
 
 
 def solution(mesh):

time: 59.8 us -> 53.7 us (0.90)
  Pallas kernels: 59.7 us -> 52.5 us
  other arithmetic: 0 us -> 1.17 us
    pallas_call x2 -> x1, Pallas kernels: 59.7 us -> 52.5 us  [shards(): pl.pallas_call(main_kernel, out_shape=pltpu.VMEM((3 * NN, LOCAL, ELEMS),...]
    transpose x0 -> x1, other arithmetic: none -> 1.17 us  [shards(): return jnp.transpose(out, (0, 2, 1, 3))]
where the time goes in v1:
time: 53.7 us
  Pallas kernels  52.5 us (98%)
  other arithmetic  1.17 us (2%)
    pallas_call x1, Pallas kernels, shards(): pl.pallas_call(main_kernel, out_shape=pltpu.VMEM((3 * NN, LOCAL, ELEMS),...  52.5 us
    transpose x1, other arithmetic, shards(): return jnp.transpose(out, (0, 2, 1, 3))  1.17 us

profile of v1, /device:TPU:1, one launch (start us, length us, event | category | flops | bytes accessed | tf_op | source)
XLA Modules:
  0.0 53.7 jit_solution(14857885770137924980)
XLA Ops:
  0.0 52.5 %advect.1 = f32[147,16,128]{2,1,0:T(8,128)S(1)} custom-call(f32[147,16,128]{2,1,0:T(8,128)} %bitcast.11, f32[49,4,128]{2,1,0:T(4,128)} %bitcast.12, f32[14,4,128]{2,1,0:T(4,128)} %bitcast.13, s32[4,128]{1,0:T(4,128)} %nb_hbm.1, s32[4,128]{1,0:T(4,128)} %ns_hbm.1, s32[4,128]{1,0:T(4,128)} %or_hbm.1, bf16[1024,1536]{1,0:T(8,128)(2,1)} %constant.20.clone.inv_hbm, ...), custom_call_target="tpu_custom_call" | custom-call | tf_op jit(solution)/shard_map/advect/pallas_call | solution.py:566
  52.5 1.2 %multiply_bitcast_fusion = f32[3,16,49,128]{3,1,2,0:T(8,128)} fusion(f32[3,49,16,128]{3,2,1,0:T(8,128)S(1)} %bitcast.10, f32[16]{0:T(128)S(1)} %compare_select_fusion), kind=kLoop, calls=%fused_computation | loop fusion | flops 301056 | bytes 2408512 | tf_op jit(solution)/shard_map/transpose | solution.py:626
  (1 shorter events, 0.0 us)

commit v2 on v1

--- a/solution.py
+++ b/solution.py
@@ -19,8 +19,7 @@
 LOCAL = 16
 ELEMS = 128
 SPAN_WAVENUMBER = 0.25
-VEL_GROUPS = 5
-GROUPS = 8
+GROUPS = 6
 
 GLL_POINTS = (
     -1.0,
@@ -34,13 +33,29 @@
 
 PIECES = (
     (0, 0, 0, 32),
-    (1, 0, 32, 17),
-    (1, 17, 130, 15),
-    (2, 0, 49, 32),
-    (3, 0, 81, 17),
-    (3, 17, 145, 2),
-    (4, 0, 98, 32),
+    (3, 0, 32, 17),
+    (3, 17, 81, 15),
+    (1, 0, 49, 32),
+    (4, 0, 130, 17),
+    (4, 17, 96, 2),
+    (2, 0, 98, 32),
 )
+TRACES = (
+    (0, 0, 13, 4, 19),
+    (0, 13, 15, 6, 0),
+    (1, 0, 28, 5, 0),
+    (2, 0, 4, 5, 28),
+    (2, 4, 16, 7, 0),
+    (2, 20, 8, 8, 0),
+)
+RETURNS = (
+    tuple(range(0, 32)),
+    tuple(range(49, 81)),
+    tuple(range(98, 130)),
+    tuple(range(32, 49)) + tuple(range(81, 96)),
+)
+HALF = tuple(range(130, 146))
+QUARTER = (146, 96, 97)
 
 
 def derivative_matrix():
@@ -86,14 +101,17 @@
                     derive[4 * (b * NP + i) + e, 256 + 4 * (j * NP + i) + e] = matrix[j, b]
     high, low = split_np(derive)
     derive = np.concatenate([high, high, low], axis=0)
-    place = np.zeros((128, 512))
-    for side in range(4):
-        for position in range(NP):
+    place = np.zeros((3, 256, 512))
+    starts = {(0, 0): 76, (0, 13): 128, (1, 0): 0, (2, 0): 112, (2, 4): 128, (2, 20): 192}
+    for comp, first, count, _, _ in TRACES:
+        for k in range(count):
+            side, position = divmod(first + k, NP)
             for e in range(4):
-                column = 4 * side_node(side, position) + e
-                place[4 * (side * NP + position) + e, 256 * (side % 2) + column] = 1.0
+                column = 256 * (side % 2) + 4 * side_node(side, position) + e
+                place[comp, starts[comp, first] + 4 * k + e, column] = 1.0
     place = place.astype(ml_dtypes.bfloat16)
-    return backward, forward, derive, np.concatenate([place, place], axis=0)
+    place[1, 128:] = place[1, :128]
+    return backward, forward, derive, np.concatenate([place, place], axis=1)
 
 
 def halves(value):
@@ -138,12 +156,19 @@
     place_hbm,
     out,
     back,
+    back_h,
+    back_q,
     done,
     vn,
     vs,
+    vp,
     sb,
+    sp,
     rx,
+    rp,
     sb2,
+    sh2,
+    sq2,
     inv,
     fwd,
     der,
@@ -170,6 +195,7 @@
     base,
     uu,
     xa,
+    pa,
     la,
     xp,
     tail,
@@ -182,11 +208,36 @@
     halo_send,
     halo_recv,
     out_sem,
+    ready_sem,
 ):
     me = lax.axis_index("mode")
     part = lax.axis_index("plane")
+    has_above = part < PLANES - 1
+    has_below = part > 0
     above = lax.rem(part + 1, PLANES)
     below = lax.rem(part + PLANES - 1, PLANES)
+
+    barrier = pltpu.get_barrier_semaphore()
+
+    @pl.loop(1, MODES)
+    def _(k):
+        pl.semaphore_signal(
+            barrier, inc=1, device_id={"mode": lax.rem(me + k, MODES)}, device_id_type=MESH
+        )
+
+    @pl.when(has_above)
+    def _():
+        pl.semaphore_signal(barrier, inc=1, device_id={"plane": above}, device_id_type=MESH)
+
+    def entered():
+        @pl.when(has_below)
+        def _():
+            pl.semaphore_wait(barrier, MODES)
+            pl.semaphore_signal(ready_sem, inc=1, device_id={"plane": below}, device_id_type=MESH)
+
+        @pl.when(part == 0)
+        def _():
+            pl.semaphore_wait(barrier, MODES - 1)
 
     nbv[...] = jnp.full((8, 128), -1, jnp.int32)
     nsv[...] = jnp.zeros((8, 128), jnp.int32)
@@ -219,20 +270,15 @@
         copy.start()
         others.append(copy)
 
-    barrier = pltpu.get_barrier_semaphore()
-
-    @pl.loop(1, MODES)
-    def _(k):
-        pl.semaphore_signal(
-            barrier, inc=1, device_id={"mode": lax.rem(me + k, MODES)}, device_id_type=MESH
-        )
-
-    for other in (above, below):
-        pl.semaphore_signal(barrier, inc=1, device_id={"plane": other}, device_id_type=MESH)
-
-    vs[3, pl.ds(19, 13)] = jnp.zeros((13, LOCAL, 128), F32)
-    for comp in range(3):
-        vs[VEL_GROUPS + comp, pl.ds(28, 4)] = jnp.zeros((4, LOCAL, 128), F32)
+    vp[...] = jnp.zeros_like(vp)
+
+    @pl.when(part == 0)
+    def _():
+        up_in[...] = jnp.zeros_like(up_in)
+
+    @pl.when(part == PLANES - 1)
+    def _():
+        dn_in[...] = jnp.zeros_like(dn_in)
 
     def scatter(group):
         @pl.loop(0, 2)
@@ -260,14 +306,42 @@
                 device_id_type=MESH,
             ).start()
 
-    for group in range(VEL_GROUPS):
+    def depart(group):
         for owner, copy in loads:
             if owner == group:
                 copy.wait()
         scatter(group)
         if group == 0:
-            pl.semaphore_wait(barrier, MODES + 1)
+            entered()
         send(group)
+
+    def part_rows(group):
+        return pl.ds(0, 4 if group == 8 else 8)
+
+    def depart_part(group):
+        k = group - GROUPS
+
+        def store(d, tile):
+            sp[k, d] = tile
+
+        lane_swap(lambda p: vp[k, p], store)
+        some = part_rows(group)
+        pltpu.make_async_copy(sp.at[k, me, some], rp.at[k, me, some], recv_sem.at[group]).start()
+
+        @pl.loop(1, MODES)
+        def _(j):
+            to = lax.rem(me + j, MODES)
+            pltpu.make_async_remote_copy(
+                src_ref=sp.at[k, to, some],
+                dst_ref=rp.at[k, me, some],
+                send_sem=send_sem.at[group],
+                recv_sem=recv_sem.at[group],
+                device_id={"mode": to},
+                device_id_type=MESH,
+            ).start()
+
+    for group in (0, 3, 1):
+        depart(group)
 
     for copy in others[:4]:
         copy.wait()
@@ -335,9 +409,8 @@
             moved = pltpu.roll(picked[k], by, 1) if by else picked[k]
             packed = moved if packed is None else jnp.where(lane < 32 * k + 32, moved, packed)
         ref[...] = packed
-    halo = []
-    for k, (src, dst, to) in enumerate(((up_out, up_in, above), (dn_out, dn_in, below))):
-        copy = pltpu.make_async_remote_copy(
+    halo = [
+        pltpu.make_async_remote_copy(
             src_ref=src,
             dst_ref=dst,
             send_sem=halo_send.at[k],
@@ -345,8 +418,17 @@
             device_id={"plane": to},
             device_id_type=MESH,
         )
-        copy.start()
-        halo.append(copy)
+        for k, (src, dst, to) in enumerate(((up_out, up_in, above), (dn_out, dn_in, below)))
+    ]
+
+    @pl.when(has_below)
+    def _():
+        halo[1].start()
+
+    @pl.when(has_above)
+    def _():
+        pl.semaphore_wait(ready_sem, 1)
+        halo[0].start()
 
     for copy in others[4:6]:
         copy.wait()
@@ -374,8 +456,14 @@
         rows[pl.ds(4 + axis, 1)] = total[0:1] + total[2:3]
         rows[pl.ds(6 + axis, 1)] = total[1:2] + total[3:4]
 
-    for copy in halo:
-        copy.wait_recv()
+    @pl.when(has_below)
+    def _():
+        halo[0].wait_recv()
+
+    @pl.when(has_above)
+    def _():
+        halo[1].wait_recv()
+
     lane1 = lax.broadcasted_iota(jnp.int32, (8, 128), 1)
     key_up = pltpu.roll(up_in[pl.ds(0, 8)], 32, 1)
     key_dn = pltpu.roll(dn_in[pl.ds(0, 8)], 64, 1)
@@ -389,22 +477,43 @@
         high, low = halves(jnp.where(lane < 32, from_up, jnp.where(lane < 64, from_dn, 0.0)))
         both = matmul_nt(jnp.concatenate([high, low], axis=0), oht[...])
         across = across + (both[:112] + both[112:])
-        for side in range(4):
-            for position in range(NP):
-                vs[VEL_GROUPS + comp, side * NP + position] = across[
-                    position * 16 : position * 16 + 16, side * 128 : side * 128 + 128
-                ]
-        scatter(VEL_GROUPS + comp)
-        send(VEL_GROUPS + comp)
+        for owner, first, count, group, slot in TRACES:
+            if owner != comp:
+                continue
+            for k in range(count):
+                side, position = divmod(first + k, NP)
+                lanes = slice(side * 128, side * 128 + 128)
+                where = slice(position * 16, position * 16 + 16)
+                if group < GROUPS:
+                    vs[group, slot + k] = across[where, lanes]
+                    continue
+                parts = 4 if group == 8 else 2
+                for part_at in range(parts):
+                    size = 16 // parts
+                    at = position * 16 + part_at * size
+                    vp[group - GROUPS, part_at * (32 // parts) + k, pl.ds(0, size)] = across[
+                        at : at + size, lanes
+                    ]
+        if comp == 0:
+            depart(4)
+            depart(2)
+            depart_part(6)
+        elif comp == 1:
+            continue
+        else:
+            depart(5)
+            depart_part(7)
+            depart_part(8)
 
     def received(group):
-        pltpu.make_async_copy(rx.at[group], rx.at[group], recv_sem.at[group]).wait()
+        ref = rx.at[group] if group < GROUPS else rp.at[group - GROUPS, :, part_rows(group)]
+        pltpu.make_async_copy(ref, ref, recv_sem.at[group]).wait()
 
     for copy in others[6:]:
         copy.wait()
     lane64 = lax.broadcasted_iota(jnp.int32, (64, 128), 1)
 
-    def on_planes(comp, pieces):
+    def gather(pieces):
         @pl.loop(0, 8)
         def _(block):
             at = pl.multiple_of(block * 64, 64)
@@ -415,8 +524,7 @@
                 xr[pl.ds(at + 512, 64), lanes] = high
                 xr[pl.ds(at + 1024, 64), lanes] = low
 
-        pv[comp] = matmul(inv[...], xr[...])
-
+    def derive(comp):
         @pl.loop(0, 8)
         def _(block):
             rows64 = pl.ds(pl.multiple_of(block * 64, 64), 64)
@@ -429,71 +537,89 @@
 
     def joined(rows64):
         return jnp.where(
-            lane64 < 60, pltpu.roll(rx[1, rows64], 60, 1), pltpu.roll(rx[3, rows64], 120, 1)
+            lane64 < 60, pltpu.roll(rx[3, rows64], 60, 1), pltpu.roll(rx[4, rows64], 120, 1)
         )
 
     received(0)
+    received(3)
+    gather((lambda r: rx[0, r], lambda r: rx[3, r]))
+    pv[0] = matmul(inv[...], xr[...])
+    derive(0)
     received(1)
-    on_planes(0, (lambda r: rx[0, r], lambda r: rx[1, r]))
+    received(4)
+    gather((lambda r: rx[1, r], joined))
+    pv[1] = matmul(inv[...], xr[...])
+    derive(1)
     received(2)
-    received(3)
-    on_planes(1, (lambda r: rx[2, r], lambda r: rx[3, r]))
-    received(4)
-    on_planes(2, (lambda r: rx[4, r], joined))
-
-    @pl.loop(0, 16)
-    def _(block):
-        at = pl.multiple_of(block * 32, 32)
-        rows32 = pl.ds(at, 32)
-        u, v, w = pv[0, rows32], pv[1, rows32], pv[2, rows32]
-        first = u * rows[pl.ds(0, 1)] + v * rows[pl.ds(1, 1)]
-        second = u * rows[pl.ds(2, 1)] + v * rows[pl.ds(3, 1)]
-        layer_a = u * rows[pl.ds(4, 1)] + v * rows[pl.ds(5, 1)]
-        layer_b = u * rows[pl.ds(6, 1)] + v * rows[pl.ds(7, 1)]
-        uu[0, rows32] = layer_a
-        uu[1, rows32] = layer_b
-        layer_b = layer_a + layer_b
-        for comp in range(3):
-            total = first * dxe[comp, rows32, pl.ds(0, 256)]
-            total = total + second * dxe[comp, rows32, pl.ds(256, 256)]
-            total = total + w * pv[comp, pl.ds(at + 512, 32)]
-            base[comp, rows32] = total - layer_b * pv[comp, rows32]
-
-    def send_back(group):
-        pltpu.make_async_copy(
-            sb2.at[group, pl.ds(pl.multiple_of(me * LOCAL, LOCAL), LOCAL)],
-            back.at[group, me],
-            recv2_sem.at[group],
-        ).start()
+    gather((lambda r: rx[2, r], lambda r: rx[4, r]))
+    pv[2, pl.ds(0, 512)] = matmul(inv[pl.ds(0, 512)], xr[...])
+
+    def bases(comps):
+        @pl.loop(0, 16)
+        def _(block):
+            at = pl.multiple_of(block * 32, 32)
+            rows32 = pl.ds(at, 32)
+            u, v, w = pv[0, rows32], pv[1, rows32], pv[2, rows32]
+            first = u * rows[pl.ds(0, 1)] + v * rows[pl.ds(1, 1)]
+            second = u * rows[pl.ds(2, 1)] + v * rows[pl.ds(3, 1)]
+            if 0 in comps:
+                uu[0, rows32] = u * rows[pl.ds(4, 1)] + v * rows[pl.ds(5, 1)]
+                uu[1, rows32] = u * rows[pl.ds(6, 1)] + v * rows[pl.ds(7, 1)]
+            layers = uu[0, rows32] + uu[1, rows32]
+            for comp in comps:
+                total = first * dxe[comp, rows32, pl.ds(0, 256)]
+                total = total + second * dxe[comp, rows32, pl.ds(256, 256)]
+                total = total + w * pv[comp, pl.ds(at + 512, 32)]
+                base[comp, rows32] = total - layers * pv[comp, rows32]
+
+    bases((0, 1))
+
+    def send_back(index, source, target):
+        pltpu.make_async_copy(source(me), target, recv2_sem.at[index]).start()
 
         @pl.loop(1, MODES)
         def _(k):
             to = lax.rem(me + k, MODES)
             pltpu.make_async_remote_copy(
-                src_ref=sb2.at[group, pl.ds(pl.multiple_of(to * LOCAL, LOCAL), LOCAL)],
-                dst_ref=back.at[group, me],
-                send_sem=send2_sem.at[group],
-                recv_sem=recv2_sem.at[group],
+                src_ref=source(to),
+                dst_ref=target,
+                send_sem=send2_sem.at[index],
+                recv_sem=recv2_sem.at[index],
                 device_id={"mode": to},
                 device_id_type=MESH,
             ).start()
 
-    @pl.loop(0, 3)
-    def _(comp):
-        received(VEL_GROUPS + comp)
-
+    def whole_back(group):
+        send_back(
+            group,
+            lambda to: sb2.at[group, pl.ds(pl.multiple_of(to * LOCAL, LOCAL), LOCAL)],
+            back.at[group, me],
+        )
+
+    def traces_on_planes(slot, load):
         @pl.loop(0, 8)
         def _(block):
             at = pl.multiple_of(block * 64, 64)
-            high, low = halves(rx[VEL_GROUPS + comp, pl.ds(at, 64)])
+            high, low = halves(load(pl.ds(at, 64)))
             xa[pl.ds(at, 64)] = high
             xa[pl.ds(at + 512, 64)] = high
             xa[pl.ds(at + 1024, 64)] = low
 
-        high, low = halves(matmul(inv[pl.ds(0, 512)], xa[...]))
-        la[:, pl.ds(0, 128)] = high
-        la[:, pl.ds(128, 128)] = low
-        dxe[0] = matmul(la[...], place[...])
+        pa[slot] = matmul(inv[pl.ds(0, 512)], xa[...])
+
+    def product(comp, loads_):
+        count = len(loads_)
+
+        @pl.loop(0, 8)
+        def _(block):
+            rows64 = pl.ds(pl.multiple_of(block * 64, 64), 64)
+            for k, load in enumerate(loads_):
+                high, low = halves(load(rows64))
+                la[rows64, pl.ds(128 * k, 128)] = high
+                la[rows64, pl.ds(128 * (count + k), 128)] = low
+
+        wide = pl.ds(0, 256 * count)
+        dxe[0] = matmul(la[:, wide], place[comp, wide])
 
         @pl.loop(0, 8)
         def _(block):
@@ -507,49 +633,127 @@
             xp[pl.ds(at + 1024, 64)] = low
 
         result = matmul(fwd[...], xp[...])
-        sb2[2 * comp] = result[:, :128]
+        sb2[comp] = result[:, :128]
         tail[comp] = result[:, 128:]
-        send_back(2 * comp)
-
-    @pl.loop(0, 8)
-    def _(block):
-        rows64 = pl.ds(pl.multiple_of(block * 64, 64), 64)
-        last = tail[2, rows64]
-        sb2[1, rows64] = jnp.where(lane64 < 68, tail[0, rows64], pltpu.roll(last, 68, 1))
-        sb2[3, rows64] = jnp.where(lane64 < 68, tail[1, rows64], pltpu.roll(last, 8, 1))
-
-    send_back(1)
-    send_back(3)
+        whole_back(comp)
+
+    def half_tiles(k):
+        tiles = rp[k][:, None]
+        return jnp.concatenate([tiles, pltpu.roll(tiles, 64, 3)], axis=1).reshape(NZ, 128)
+
+    received(6)
+    rx[6] = half_tiles(0)
+    traces_on_planes(0, lambda r: rx[6, r])
+    product(0, (lambda r: pv[2, r, pl.ds(128, 128)], lambda r: pa[0, r]))
+    received(5)
+    traces_on_planes(1, lambda r: rx[5, r])
+    product(1, (lambda r: pa[1, r],))
+    lane512 = lax.broadcasted_iota(jnp.int32, (512, 128), 1)
+    sb2[3] = jnp.where(lane512 < 68, tail[0], pltpu.roll(tail[1], 68, 1))
+    whole_back(3)
+    pv[2, pl.ds(512, 512)] = matmul(inv[pl.ds(512, 512)], xr[...])
+    derive(2)
+    bases((2,))
+    received(7)
+    received(8)
+    low_rows = lax.broadcasted_iota(jnp.int32, (MODES, 8, 128), 1) < 4
+    tiles = rp[2]
+    pairs = []
+    for even, odd in ((64, 32), (0, 96)):
+        upper = pltpu.roll(pltpu.roll(tiles, odd, 2), 4, 1)
+        lower = pltpu.roll(tiles, even, 2) if even else tiles
+        pairs.append(jnp.where(low_rows, lower, upper)[:, None])
+    quarter = jnp.concatenate(pairs, axis=1).reshape(NZ, 128)
+    rx[6] = jnp.where(lane512 < 64, half_tiles(1), jnp.where(lane512 < 96, quarter, 0.0))
+    traces_on_planes(0, lambda r: rx[6, r])
+    product(2, (lambda r: pa[1, r], lambda r: pa[0, r]))
+    lane3 = lax.broadcasted_iota(jnp.int32, (MODES, 8, 128), 2)
+    ends = tail[2].reshape(MODES, 2, 8, 128)
+    sh2[...] = jnp.where(lane3 < 64, ends[:, 0], pltpu.roll(ends[:, 1], 64, 2))
+    send_back(4, lambda to: sh2.at[to], back_h.at[me])
+
+    others1 = tail[1].reshape(MODES, 2, 8, 128)
+    packed = None
+    for k in (1, 0):
+        end = jnp.where(lane3 < 4, pltpu.roll(ends[:, k], 64, 2), pltpu.roll(others1[:, k], 72, 2))
+        for upper in (1, 0):
+            block = 2 * k + upper
+            moved = pltpu.roll(end, 4, 1) if upper else end
+            moved = pltpu.roll(moved, 32 * block, 2) if block else moved
+            packed = moved if packed is None else jnp.where(lane3 < 32 * block + 32, moved, packed)
+    sq2[...] = packed
+    few = pl.ds(0, 4)
+    send_back(5, lambda to: sq2.at[to, few], back_q.at[me, few])
 
     leaving = []
-    for group in (0, 2, 4, 1, 3):
-        pltpu.make_async_copy(back.at[group], back.at[group], recv2_sem.at[group]).wait()
+
+    def leave(first, count):
+        copy = pltpu.make_async_copy(
+            done.at[pl.ds(first, count)], out.at[pl.ds(first, count)], out_sem.at[len(leaving)]
+        )
+        copy.start()
+        leaving.append(copy)
+
+    def arrived(index, ref):
+        pltpu.make_async_copy(ref, ref, recv2_sem.at[index]).wait()
+
+    for group, parts in (
+        (0, ((0, 32),)),
+        (1, ((49, 32),)),
+        (3, ((32, 17), (81, 15))),
+        (2, ((98, 32),)),
+    ):
+        arrived(group, back.at[group])
 
         @pl.loop(0, 2)
         def _(half):
             rows8 = pl.ds(pl.multiple_of(half * 8, 8), 8)
 
             def store(d, tile):
-                done[group, d, rows8] = tile
+                done[RETURNS[group][d], rows8] = tile
 
             lane_swap(lambda p: back[group, p, rows8], store)
 
-        for k, (owner, slot, row, count) in enumerate(PIECES):
-            if owner == group:
-                copy = pltpu.make_async_copy(
-                    done.at[group, pl.ds(slot, count)], out.at[pl.ds(row, count)], out_sem.at[k]
-                )
-                copy.start()
-                leaving.append(copy)
-
-    for copy in halo:
-        copy.wait_send()
+        for span in parts:
+            leave(*span)
+
+    def store_half(d, tile):
+        done[HALF[d % 16], pl.ds(d // 16 * 8, 8)] = tile
+
+    arrived(4, back_h)
+    lane_swap(lambda p: back_h[p], store_half)
+    leave(130, 16)
+
+    def store_last(d, tile):
+        if d % 8 < len(QUARTER):
+            done[QUARTER[d % 8], pl.ds(d // 8 * 4, 4)] = tile[:4]
+
+    arrived(5, back_q.at[:, few])
+    lane_swap(lambda p: back_q[p], store_last)
+    leave(96, 2)
+    leave(146, 1)
+
+    @pl.when(has_above)
+    def _():
+        halo[0].wait_send()
+
+    @pl.when(has_below)
+    def _():
+        halo[1].wait_send()
+
     for group in range(GROUPS):
         sent = sb.at[group, pl.ds(0, MODES - 1)]
         pltpu.make_async_copy(sent, sent, send_sem.at[group]).wait()
-    for group in range(VEL_GROUPS):
+    for k in range(3):
+        sent = sp.at[k, pl.ds(0, MODES - 1), part_rows(GROUPS + k)]
+        pltpu.make_async_copy(sent, sent, send_sem.at[GROUPS + k]).wait()
+    for group in range(4):
         sent = sb2.at[group, pl.ds(0, (MODES - 1) * LOCAL)]
         pltpu.make_async_copy(sent, sent, send2_sem.at[group]).wait()
+    sent = sh2.at[pl.ds(0, MODES - 1)]
+    pltpu.make_async_copy(sent, sent, send2_sem.at[4]).wait()
+    sent = sq2.at[pl.ds(0, MODES - 1), few]
+    pltpu.make_async_copy(sent, sent, send2_sem.at[5]).wait()
     for copy in leaving:
         copy.wait()
 
@@ -569,17 +773,24 @@
         in_specs=[anywhere] * 10,
         out_specs=anywhere,
         scratch_shapes=[
-            vmem((VEL_GROUPS, MODES, LOCAL, 128), F32),
-            vmem((VEL_GROUPS, 32, LOCAL, 128), F32),
+            vmem((4, MODES, LOCAL, 128), F32),
+            vmem((MODES, 8, 128), F32),
+            vmem((MODES, 8, 128), F32),
+            vmem((3 * NN, LOCAL, 128), F32),
             vmem((3 * NN, LOCAL, 128), F32),
             vmem((GROUPS, 32, LOCAL, 128), F32),
+            vmem((3, 32, 8, 128), F32),
             vmem((GROUPS, MODES, LOCAL, 128), F32),
-            vmem((GROUPS, NZ, 128), F32),
-            vmem((VEL_GROUPS, NZ, 128), F32),
+            vmem((3, MODES, 8, 128), F32),
+            vmem((GROUPS + 1, NZ, 128), F32),
+            vmem((3, MODES, 8, 128), F32),
+            vmem((4, NZ, 128), F32),
+            vmem((MODES, 8, 128), F32),
+            vmem((MODES, 8, 128), F32),
             vmem((2 * NZ, 3 * NZ), BF16),
             vmem((NZ, 3 * NZ), BF16),
             vmem((768, 512), BF16),
-            vmem((256, 512), BF16),
+            vmem((3, 512, 512), BF16),
             vmem((NN, 8, 128), F32),
             vmem((2 * NP, 8, 128), F32),
             vmem((8, 128), jnp.int32),
@@ -602,18 +813,20 @@
             vmem((3, NZ, 256), F32),
             vmem((2, NZ, 256), F32),
             vmem((3 * NZ, 128), BF16),
-            vmem((NZ, 256), BF16),
+            vmem((2, NZ, 128), F32),
+            vmem((NZ, 512), BF16),
             vmem((3 * NZ, 256), BF16),
             vmem((3, NZ, 128), F32),
             dma((len(PIECES),)),
             dma((10,)),
-            dma((GROUPS,)),
-            dma((GROUPS,)),
-            dma((VEL_GROUPS,)),
-            dma((VEL_GROUPS,)),
+            dma((GROUPS + 3,)),
+            dma((GROUPS + 3,)),
+            dma((6,)),
+            dma((6,)),
             dma((2,)),
             dma((2,)),
-            dma((len(PIECES),)),
+            dma((8,)),
+            pltpu.SemaphoreType.REGULAR,
         ],
         compiler_params=pltpu.CompilerParams(
             collective_id=0, has_side_effects=True, vmem_limit_bytes=48 << 20

time: 53.7 us -> 49.7 us (0.926)
  Pallas kernels: 52.5 us -> 48.4 us
    pallas_call x1, Pallas kernels: 52.5 us -> 48.4 us  [shards(): pl.pallas_call(main_kernel, out_shape=pltpu.VMEM((3 * NN, LOCAL, ELEMS),...]
where the time goes in v2:
time: 49.7 us; the launch traced here: 49.6 us
  Pallas kernels  48.4 us (97%)
  other arithmetic  1.17 us (2%)
    pallas_call x1, Pallas kernels, shards(): pl.pallas_call(main_kernel, out_shape=pltpu.VMEM((3 * NN, LOCAL, ELEMS),...  48.4 us
    transpose x1, other arithmetic, shards(): return jnp.transpose(out, (0, 2, 1, 3))  1.17 us

profile of v2, /device:TPU:1, one launch (start us, length us, event | category | flops | bytes accessed | tf_op | source)
XLA Modules:
  0.0 49.6 jit_solution(364889424903413441)
XLA Ops:
  0.0 48.4 %advect.1 = f32[147,16,128]{2,1,0:T(8,128)S(1)} custom-call(f32[147,16,128]{2,1,0:T(8,128)} %bitcast.11, f32[49,4,128]{2,1,0:T(4,128)} %bitcast.12, f32[14,4,128]{2,1,0:T(4,128)} %bitcast.13, s32[4,128]{1,0:T(4,128)} %nb_hbm.1, s32[4,128]{1,0:T(4,128)} %ns_hbm.1, s32[4,128]{1,0:T(4,128)} %or_hbm.1, bf16[1024,1536]{1,0:T(8,128)(2,1)} %constant.20.clone.inv_hbm, ...), custom_call_target="tpu_custom_call" | custom-call | tf_op jit(solution)/shard_map/advect/pallas_call | solution.py:770
  48.4 1.2 %multiply_bitcast_fusion = f32[3,16,49,128]{3,1,2,0:T(8,128)} fusion(f32[3,49,16,128]{3,2,1,0:T(8,128)S(1)} %bitcast.10, f32[16]{0:T(128)S(1)} %compare_select_fusion), kind=kLoop, calls=%fused_computation | loop fusion | flops 301056 | bytes 2408512 | tf_op jit(solution)/shard_map/transpose | solution.py:839
  (1 shorter events, 0.0 us)

commit v3 on v2

--- a/solution.py
+++ b/solution.py
@@ -154,11 +154,10 @@
     fwd_hbm,
     der_hbm,
     place_hbm,
-    out,
+    done,
     back,
     back_h,
     back_q,
-    done,
     vn,
     vs,
     vp,
@@ -207,7 +206,6 @@
     recv2_sem,
     halo_send,
     halo_recv,
-    out_sem,
     ready_sem,
 ):
     me = lax.axis_index("mode")
@@ -219,7 +217,7 @@
 
     barrier = pltpu.get_barrier_semaphore()
 
-    @pl.loop(1, MODES)
+    @pl.loop(1, MODES, unroll=True)
     def _(k):
         pl.semaphore_signal(
             barrier, inc=1, device_id={"mode": lax.rem(me + k, MODES)}, device_id_type=MESH
@@ -577,7 +575,7 @@
     def send_back(index, source, target):
         pltpu.make_async_copy(source(me), target, recv2_sem.at[index]).start()
 
-        @pl.loop(1, MODES)
+        @pl.loop(1, MODES, unroll=True)
         def _(k):
             to = lax.rem(me + k, MODES)
             pltpu.make_async_remote_copy(
@@ -685,24 +683,10 @@
     few = pl.ds(0, 4)
     send_back(5, lambda to: sq2.at[to, few], back_q.at[me, few])
 
-    leaving = []
-
-    def leave(first, count):
-        copy = pltpu.make_async_copy(
-            done.at[pl.ds(first, count)], out.at[pl.ds(first, count)], out_sem.at[len(leaving)]
-        )
-        copy.start()
-        leaving.append(copy)
-
     def arrived(index, ref):
         pltpu.make_async_copy(ref, ref, recv2_sem.at[index]).wait()
 
-    for group, parts in (
-        (0, ((0, 32),)),
-        (1, ((49, 32),)),
-        (3, ((32, 17), (81, 15))),
-        (2, ((98, 32),)),
-    ):
+    for group in (0, 1, 3, 2):
         arrived(group, back.at[group])
 
         @pl.loop(0, 2)
@@ -714,15 +698,11 @@
 
             lane_swap(lambda p: back[group, p, rows8], store)
 
-        for span in parts:
-            leave(*span)
-
     def store_half(d, tile):
         done[HALF[d % 16], pl.ds(d // 16 * 8, 8)] = tile
 
     arrived(4, back_h)
     lane_swap(lambda p: back_h[p], store_half)
-    leave(130, 16)
 
     def store_last(d, tile):
         if d % 8 < len(QUARTER):
@@ -730,8 +710,6 @@
 
     arrived(5, back_q.at[:, few])
     lane_swap(lambda p: back_q[p], store_last)
-    leave(96, 2)
-    leave(146, 1)
 
     @pl.when(has_above)
     def _():
@@ -754,8 +732,6 @@
     pltpu.make_async_copy(sent, sent, send2_sem.at[4]).wait()
     sent = sq2.at[pl.ds(0, MODES - 1), few]
     pltpu.make_async_copy(sent, sent, send2_sem.at[5]).wait()
-    for copy in leaving:
-        copy.wait()
 
 
 def shards(velocity, metric_terms, lift_scale, neighbour, neighbour_side, orientation):
@@ -771,12 +747,11 @@
         main_kernel,
         out_shape=pltpu.VMEM((3 * NN, LOCAL, ELEMS), F32),
         in_specs=[anywhere] * 10,
-        out_specs=anywhere,
+        out_specs=pl.BlockSpec(memory_space=vmem),
         scratch_shapes=[
             vmem((4, MODES, LOCAL, 128), F32),
             vmem((MODES, 8, 128), F32),
             vmem((MODES, 8, 128), F32),
-            vmem((3 * NN, LOCAL, 128), F32),
             vmem((3 * NN, LOCAL, 128), F32),
             vmem((GROUPS, 32, LOCAL, 128), F32),
             vmem((3, 32, 8, 128), F32),
@@ -825,7 +800,6 @@
             dma((6,)),
             dma((2,)),
             dma((2,)),
-            dma((8,)),
             pltpu.SemaphoreType.REGULAR,
         ],
         compiler_params=pltpu.CompilerParams(

time: 49.7 us -> 48.8 us (0.982)
  Pallas kernels: 48.4 us -> 47.5 us
    pallas_call x1, Pallas kernels: 48.4 us -> 47.5 us  [shards(): pl.pallas_call(main_kernel, out_shape=pltpu.VMEM((3 * NN, LOCAL, ELEMS),...]
where the time goes in v3:
time: 48.8 us; the launch traced here: 48.7 us
  Pallas kernels  47.5 us (97%)
  other arithmetic  1.17 us (2%)
    pallas_call x1, Pallas kernels, shards(): pl.pallas_call(main_kernel, out_shape=pltpu.VMEM((3 * NN, LOCAL, ELEMS),...  47.5 us
    transpose x1, other arithmetic, shards(): return jnp.transpose(out, (0, 2, 1, 3))  1.17 us

profile of v3, /device:TPU:1, one launch (start us, length us, event | category | flops | bytes accessed | tf_op | source)
XLA Modules:
  0.0 48.7 jit_solution(13681757896710217283)
XLA Ops:
  0.0 47.5 %advect.1 = f32[147,16,128]{2,1,0:T(8,128)S(1)} custom-call(f32[147,16,128]{2,1,0:T(8,128)} %bitcast.11, f32[49,4,128]{2,1,0:T(4,128)} %bitcast.12, f32[14,4,128]{2,1,0:T(4,128)} %bitcast.13, s32[4,128]{1,0:T(4,128)} %nb_hbm.1, s32[4,128]{1,0:T(4,128)} %ns_hbm.1, s32[4,128]{1,0:T(4,128)} %or_hbm.1, bf16[1024,1536]{1,0:T(8,128)(2,1)} %constant.20.clone.inv_hbm, ...), custom_call_target="tpu_custom_call" | custom-call | tf_op jit(solution)/shard_map/advect/pallas_call | solution.py:746
  47.5 1.2 %multiply_bitcast_fusion = f32[3,16,49,128]{3,1,2,0:T(8,128)} fusion(f32[3,49,16,128]{3,2,1,0:T(8,128)S(1)} %bitcast.10, f32[16]{0:T(128)S(1)} %compare_select_fusion), kind=kLoop, calls=%fused_computation | loop fusion | flops 301056 | bytes 2408512 | tf_op jit(solution)/shard_map/transpose | solution.py:813
  (1 shorter events, 0.0 us)

commit v4 on v3

--- a/solution.py
+++ b/solution.py
@@ -89,7 +89,8 @@
     slope = slope * np.where(sine_row, np.cos(phase), -np.sin(phase))
     high, low = split_np(np.concatenate([inverse.T, slope.T], axis=0))
     backward = np.concatenate([high, low, high], axis=1)
-    high, low = split_np(inverse)
+    weighting = np.where(index < 2, 1.0, 2.0) / NZ
+    high, low = split_np(inverse * weighting[:, None])
     forward = np.concatenate([high, low, high], axis=1)
     matrix = derivative_matrix()
     derive = np.zeros((256, 512))
@@ -570,7 +571,7 @@
                 total = total + w * pv[comp, pl.ds(at + 512, 32)]
                 base[comp, rows32] = total - layers * pv[comp, rows32]
 
-    bases((0, 1))
+    bases((0,))
 
     def send_back(index, source, target):
         pltpu.make_async_copy(source(me), target, recv2_sem.at[index]).start()
@@ -643,6 +644,7 @@
     rx[6] = half_tiles(0)
     traces_on_planes(0, lambda r: rx[6, r])
     product(0, (lambda r: pv[2, r, pl.ds(128, 128)], lambda r: pa[0, r]))
+    bases((1,))
     received(5)
     traces_on_planes(1, lambda r: rx[5, r])
     product(1, (lambda r: pa[1, r],))
@@ -807,9 +809,7 @@
         ),
         name="advect",
     )(*[pltpu.with_memory_space_constraint(x, pltpu.HBM) for x in operands])
-    index = lax.axis_index("mode") * LOCAL + jnp.arange(LOCAL, dtype=jnp.int32)
-    weighting = jnp.where(index < 2, 1.0 / NZ, 2.0 / NZ).astype(F32)
-    out = out.reshape(3, NN, LOCAL, ELEMS) * weighting[:, None]
+    out = out.reshape(3, NN, LOCAL, ELEMS)
     return jnp.transpose(out, (0, 2, 1, 3))
 
 

time: 48.8 us -> 48.7 us (level)
  other arithmetic: 1.17 us -> 0 us
  local copies, waits for them, and re-layouts: 0 us -> 1.02 us
    transpose x1 -> x0, other arithmetic: 1.17 us -> none  [shards(): return jnp.transpose(out, (0, 2, 1, 3))]
    unnamed x0 -> x1, local copies, waits for them, and re-layouts: none -> 1.02 us
where the time goes in v4:
time: 48.7 us; the launch traced here: 48.6 us
  Pallas kernels  47.6 us (98%)
  local copies, waits for them, and re-layouts  1.02 us (2%)
    pallas_call x1, Pallas kernels, shards(): pl.pallas_call(main_kernel, out_shape=pltpu.VMEM((3 * NN, LOCAL, ELEMS),...  47.6 us
    unnamed x1, local copies, waits for them, and re-layouts  1.02 us

profile of v4, /device:TPU:1, one launch (start us, length us, event | category | flops | bytes accessed | tf_op | source)
XLA Modules:
  0.0 48.6 jit_solution(7981129030678420045)
XLA Ops:
  0.0 47.6 %advect.1 = f32[147,16,128]{2,1,0:T(8,128)S(1)} custom-call(f32[147,16,128]{2,1,0:T(8,128)} %bitcast.11, f32[49,4,128]{2,1,0:T(4,128)} %bitcast.12, f32[14,4,128]{2,1,0:T(4,128)} %bitcast.13, s32[4,128]{1,0:T(4,128)} %nb_hbm.1, s32[4,128]{1,0:T(4,128)} %ns_hbm.1, s32[4,128]{1,0:T(4,128)} %or_hbm.1, bf16[1024,1536]{1,0:T(8,128)(2,1)} %constant.8.clone.inv_hbm, ...), custom_call_target="tpu_custom_call" | custom-call | tf_op jit(solution)/shard_map/advect/pallas_call | solution.py:748
  47.6 1.0 %copy.12 = f32[3,16,49,128]{3,1,2,0:T(8,128)} copy(f32[3,16,49,128]{3,1,2,0:T(8,128)S(1)} %bitcast.10) | data formatting | bytes 2408448
